TPU v7x, 512 devices: a whole 4x8x8 slice. The times are simulated.
512 devices in a mesh: lat: 16 (over x, y_hi), lon: 32 (over z, y_lo, core).
Axes of the slice: x: 4, y: 8 (y_hi: 4, y_lo: 2; y = y_hi * 2 + y_lo), z: 8, core: 2. Of those that a mesh axis runs over, the one named last changes fastest.
Arguments:
- inputs: bfloat16 [512, 512, 256], P('lat', 'lon'), may hold values from -6 to 6
- cotangent: bfloat16 [512, 512, 256], P('lat', 'lon'), may hold values from -6 to 6
- spectral_fine: float32 [32, 64, 2, 256, 256], P('lat', 'lon'), may hold values from -0.25 to 0.25
- spectral_coarse: float32 [16, 32, 2, 256, 256], P('lat', 'lon'), may hold values from -0.25 to 0.25
- weight_in: bfloat16 [256, 1024], replicated, may hold values from -0.375 to 0.375
- weight_out: bfloat16 [1024, 256], replicated, may hold values from -0.1875 to 0.1875
Outputs:
- output: bfloat16 [512, 512, 256], P('lat', 'lon')
- grad_inputs: bfloat16 [512, 512, 256], P('lat', 'lon')
All inputs are finite; a program needn't handle non-finite values.
Results may differ from a plain program's by a relative error of at most 0.017.
Values may be sent and summed in bfloat16 or wider, within the bound.
A program may use at most 64 MiB of HBM per device.

v0:
```python
from functools import partial
import math

import jax
import jax.numpy as jnp
from jax import lax
from jax.sharding import PartitionSpec as P

highest = lax.Precision.HIGHEST


def mode_table(mode_ids, positions, modulus):
    product = mode_ids[:, None] * positions[None, :] % modulus
    angles = product.astype(jnp.float32) * (2.0 * math.pi / modulus)
    return (jnp.cos(angles), jnp.sin(angles))


def centered(number):
    return jnp.arange(number, dtype=jnp.int32) - number // 2


def counting(number, first_index):
    return first_index + jnp.arange(number, dtype=jnp.int32)


def lat_forward(grid_field, cos_lat, sin_lat):
    real_part = jnp.einsum("jh,hwc->jwc", cos_lat, grid_field, precision=highest)
    imag_part = -jnp.einsum("jh,hwc->jwc", sin_lat, grid_field, precision=highest)
    return jnp.stack([real_part, imag_part])


def lon_forward(mode_segment, cos_lon, sin_lon):
    real_part = jnp.einsum("kw,jwc->jkc", cos_lon, mode_segment[0], precision=highest) + jnp.einsum(
        "kw,jwc->jkc", sin_lon, mode_segment[1], precision=highest
    )
    imag_part = jnp.einsum("kw,jwc->jkc", cos_lon, mode_segment[1], precision=highest) - jnp.einsum(
        "kw,jwc->jkc", sin_lon, mode_segment[0], precision=highest
    )
    return jnp.stack([real_part, imag_part])


def lon_backward(spectrum, cos_lon, sin_lon):
    real_part = jnp.einsum("kw,jko->jwo", cos_lon, spectrum[0], precision=highest) - jnp.einsum(
        "kw,jko->jwo", sin_lon, spectrum[1], precision=highest
    )
    imag_part = jnp.einsum("kw,jko->jwo", sin_lon, spectrum[0], precision=highest) + jnp.einsum(
        "kw,jko->jwo", cos_lon, spectrum[1], precision=highest
    )
    return jnp.stack([real_part, imag_part])


def lat_backward(mode_segment, cos_lat, sin_lat):
    return jnp.einsum("jh,jwo->hwo", cos_lat, mode_segment[0], precision=highest) - jnp.einsum(
        "jh,jwo->hwo", sin_lat, mode_segment[1], precision=highest
    )


def mix_modes(spectrum, weights):
    weight_real = weights[:, :, 0]
    weight_imag = weights[:, :, 1]
    real_part = jnp.einsum(
        "jki,jkio->jko", spectrum[0], weight_real, precision=highest
    ) - jnp.einsum("jki,jkio->jko", spectrum[1], weight_imag, precision=highest)
    imag_part = jnp.einsum(
        "jki,jkio->jko", spectrum[0], weight_imag, precision=highest
    ) + jnp.einsum("jki,jkio->jko", spectrum[1], weight_real, precision=highest)
    return jnp.stack([real_part, imag_part])


def mix_adjoint(spectrum, weights):
    weight_real = weights[:, :, 0]
    weight_imag = weights[:, :, 1]
    real_part = jnp.einsum(
        "jko,jkio->jki", spectrum[0], weight_real, precision=highest
    ) + jnp.einsum("jko,jkio->jki", spectrum[1], weight_imag, precision=highest)
    imag_part = jnp.einsum(
        "jko,jkio->jki", spectrum[1], weight_real, precision=highest
    ) - jnp.einsum("jko,jkio->jki", spectrum[0], weight_imag, precision=highest)
    return jnp.stack([real_part, imag_part])


def shrink(grid_field):
    height, width, depth = grid_field.shape
    return grid_field.reshape(height // 2, 2, width // 2, 2, depth).sum(axis=(1, 3))


def expand(grid_field):
    return jnp.repeat(jnp.repeat(grid_field, 2, axis=0), 2, axis=1)


def feed_forward(mixed, cotangent, weight_in, weight_out):
    hidden = jnp.dot(mixed, weight_in, preferred_element_type=jnp.float32)
    activated, pullback = jax.vjp(partial(jax.nn.gelu, approximate=True), hidden)
    output = (
        mixed.astype(jnp.float32)
        + jnp.dot(activated.astype(jnp.bfloat16), weight_out, preferred_element_type=jnp.float32)
    ).astype(jnp.bfloat16)
    d_act = jnp.dot(cotangent, weight_out.T, preferred_element_type=jnp.float32)
    d_hidden = pullback(d_act)[0].astype(jnp.bfloat16)
    d_mixed = (
        cotangent.astype(jnp.float32)
        + jnp.dot(d_hidden, weight_in.T, preferred_element_type=jnp.float32)
    ).astype(jnp.bfloat16)
    return (output, d_mixed)


def fine_analysis(low_field, tables, factor):
    mode_segment = lax.psum_scatter(
        lat_forward(low_field.astype(jnp.float32), *tables[0]),
        "lat",
        scatter_dimension=1,
        tiled=True,
    )
    spectrum = lax.psum_scatter(
        lon_forward(mode_segment, *tables[1]), "lon", scatter_dimension=2, tiled=True
    )
    return spectrum * factor


def coarse_analysis(grid_field, tables, factor):
    mode_segment = lax.psum_scatter(
        lat_forward(grid_field, *tables[0]).astype(jnp.bfloat16),
        "lat",
        scatter_dimension=1,
        tiled=True,
    ).astype(jnp.float32)
    spectrum = lax.psum_scatter(
        lon_forward(mode_segment, *tables[1]).astype(jnp.bfloat16),
        "lon",
        scatter_dimension=2,
        tiled=True,
    ).astype(jnp.float32)
    return spectrum * factor


def mode_adder(tables, mode_piece):
    cos_lat, sin_lat = tables[0]
    return lat_backward(mode_piece, cos_lat, sin_lat)


def fine_synthesis(spectrum, tables, factor):
    gathered = lax.all_gather(spectrum, "lon", axis=2, tiled=True)
    mode_segment = lon_backward(gathered, *tables[1])
    result = mode_adder(tables, lax.all_gather(mode_segment, "lat", axis=1, tiled=True))
    return result * factor


def coarse_synthesis(spectrum, tables, factor):
    gathered = lax.all_gather(spectrum, "lon", axis=2, tiled=True)
    mode_segment = lon_backward(gathered, *tables[1])
    result = mode_adder(tables, lax.all_gather(mode_segment, "lat", axis=1, tiled=True))
    return result * factor


def local(inputs, cotangent, spectral_fine, spectral_coarse, weight_in, weight_out):
    row_count, column_count, channel_count = inputs.shape
    lat_devices = lax.axis_size("lat")
    lon_devices = lax.axis_size("lon")
    grid_rows = row_count * lat_devices
    grid_columns = column_count * lon_devices
    row_first = lax.axis_index("lat") * row_count
    column_first = lax.axis_index("lon") * column_count
    fine_lat = spectral_fine.shape[0] * lat_devices
    fine_lon = spectral_fine.shape[1] * lon_devices
    coarse_lat = spectral_coarse.shape[0] * lat_devices
    coarse_lon = spectral_coarse.shape[1] * lon_devices
    fine_tables = (
        mode_table(centered(fine_lat), counting(row_count, row_first), grid_rows),
        mode_table(
            jnp.arange(fine_lon, dtype=jnp.int32),
            counting(column_count, column_first),
            grid_columns,
        ),
    )
    coarse_tables = (
        mode_table(centered(coarse_lat), counting(row_count // 2, row_first // 2), grid_rows // 2),
        mode_table(
            jnp.arange(coarse_lon, dtype=jnp.int32),
            counting(column_count // 2, column_first // 2),
            grid_columns // 2,
        ),
    )
    fine_in = 1.0 / math.sqrt(grid_rows * grid_columns)
    fine_out = 1.0 / math.sqrt(fine_lat * fine_lon)
    coarse_in = 1.0 / math.sqrt(grid_rows * grid_columns / 4)
    coarse_out = 1.0 / math.sqrt(coarse_lat * coarse_lon)
    fine_shape = (row_count, column_count, channel_count)
    whole_input = inputs.astype(jnp.float32)
    fine_spectrum = mix_modes(fine_analysis(inputs, fine_tables, fine_in), spectral_fine)
    fine_branch = fine_synthesis(fine_spectrum, fine_tables, fine_out)
    coarse = shrink(whole_input) * 0.25
    coarse_spectrum = mix_modes(coarse_analysis(coarse, coarse_tables, coarse_in), spectral_coarse)
    coarse_branch = coarse_synthesis(coarse_spectrum, coarse_tables, coarse_out)
    mixed = (whole_input + fine_branch + expand(coarse_branch)).astype(jnp.bfloat16)
    flat_output, flat_back = feed_forward(
        mixed.reshape(-1, channel_count),
        cotangent.reshape(-1, channel_count),
        weight_in,
        weight_out,
    )
    output = flat_output.reshape(fine_shape)
    d_mixed = flat_back.reshape(fine_shape)
    back_input = d_mixed.astype(jnp.float32)
    back_spectrum = mix_adjoint(fine_analysis(d_mixed, fine_tables, fine_out), spectral_fine)
    back_fine = fine_synthesis(back_spectrum, fine_tables, fine_in)
    back_low = mix_adjoint(
        coarse_analysis(shrink(back_input), coarse_tables, coarse_out), spectral_coarse
    )
    back_coarse = coarse_synthesis(back_low, coarse_tables, coarse_in)
    grad_inputs = (back_input + back_fine + 0.25 * expand(back_coarse)).astype(jnp.bfloat16)
    return (output, grad_inputs)


def solution(mesh):
    placed = (
        P("lat", "lon", None),
        P("lat", "lon", None),
        P("lat", "lon", None, None, None),
        P("lat", "lon", None, None, None),
        P(),
        P(),
    )
    return jax.shard_map(
        local,
        mesh=mesh,
        in_specs=placed,
        out_specs=(P("lat", "lon", None), P("lat", "lon", None)),
        check_vma=False,
    )
```

profile of v0, /device:TPU:1, one launch (start us, length us, event | category | flops | bytes accessed | tf_op | source)
XLA Modules:
  0.0 1135.4 jit_solution(4370976872635772113)
XLA Ops:
  7.3 1.1 copy_convert_fusion
  12.0 1.6 copy.76
  13.7 1.5 dynamic-slice
  15.9 90.9 %reduce-scatter.9.cloned.1.call-done = bf16[2,1,8,256]{3,2,0,1:T(8,128)(2,1)} async-done(((bf16[2,16,8,256]{3,2,0,1:T(8,128)(2,1)}), bf16[2,1,8,256]{3,2,0,1:T(8,128)(2,1)}) %reduce-scatter.9.cloned.1.call-update) | async-done | bytes 8208 | tf_op jit(solution)/shard_map/reduce_scatter | solution.py:121
  107.7 0.9 fusion.43
  108.6 0.9 fusion.215
  109.5 0.9 fusion.44
  110.5 104.9 %all-reduce.1 = bf16[2,1,32,256]{3,0,1,2:T(2,128)(2,1)S(1)} all-reduce(bf16[2,1,32,256]{3,0,1,2:T(2,128)(2,1)S(1)} %copy.88), channel_id=5, replica_groups=mesh['lat'=16,'lon'=32] {'lon'}, use_global_device_ids=true, to_apply=%region_4.5.clone | all-reduce | flops 16384 | bytes 65536
  216.5 1.2 fusion.145
  217.7 1.2 fusion.144
  218.9 1.2 fusion.25
  220.1 1.2 fusion.26
  222.6 228.6 %all-reduce.7.cloned.1.call-done = f32[2,2,64,256]{3,2,1,0:T(8,128)} async-done(((f32[2,2,64,256]{3,2,1,0:T(8,128)}), f32[2,2,64,256]{3,2,1,0:T(8,128)}) %all-reduce.7.cloned.1.call-update) | async-done | bytes 262160
  454.4 32.1 %all_gather.24 = f32[2,2,64,256]{3,1,0,2:T(2,128)S(1)} all-gather(f32[2,2,2,256]{3,1,0,2:T(2,128)S(1)} %pad_maximum_fusion.12), channel_id=1, replica_groups=mesh['lat'=16,'lon'=32] {'lon'}, dimensions={2}, use_global_device_ids=true | all-gather | bytes 270336 | tf_op jit(solution)/shard_map/all_gather | solution.py:142
  488.4 32.3 %all_gather.26 = f32[2,1,32,256]{3,0,1,2:T(2,128)S(1)} all-gather(f32[2,1,1,256]{3,0,1,2:T(2,128)S(1)} %pad_maximum_fusion.14), channel_id=1, replica_groups=mesh['lat'=16,'lon'=32] {'lon'}, dimensions={2}, use_global_device_ids=true | all-gather | bytes 67584 | tf_op jit(solution)/shard_map/all_gather | solution.py:149
  522.0 38.1 %all_gather.27 = f32[2,16,8,256]{3,2,1,0:T(8,128)S(1)} all-gather(f32[2,1,8,256]{3,2,1,0:T(8,128)S(1)} %pad_maximum_fusion.10), channel_id=1, replica_groups=mesh['lat'=16,'lon'=32] {'lat'}, dimensions={1}, use_global_device_ids=true | all-gather | bytes 278528 | tf_op jit(solution)/shard_map/all_gather | solution.py:151
  561.7 1.8 reshape.280
  563.5 1.3 slice_bitcast_fusion.2
  564.8 1.0 fusion.86
  565.9 1.1 fusion.18
  567.1 1.8 fusion.486
  568.9 3.5 fusion.20
  572.4 1.1 reshape.292
  573.5 1.4 reduce_sum.19
  575.8 2.0 fusion.9
  578.6 1.2 convolution_bitcast_fusion
  579.8 1.1 pad_maximum_fusion.1
  580.9 1.6 copy.97
  582.6 3.3 fusion.17
  585.9 82.2 %reduce-scatter.13.cloned.1.call-done = bf16[2,1,8,256]{3,2,0,1:T(8,128)(2,1)} async-done(((bf16[2,16,8,256]{3,2,0,1:T(8,128)(2,1)}), bf16[2,1,8,256]{3,2,0,1:T(8,128)(2,1)}) %reduce-scatter.13.cloned.1.call-update) | async-done | bytes 8208 | tf_op jit(solution)/shard_map/reduce_scatter | solution.py:121
  668.1 0.9 fusion.207
  670.8 0.9 fusion.42
  671.8 106.1 %all-reduce.3 = bf16[2,1,32,256]{3,0,1,2:T(2,128)(2,1)S(1)} all-reduce(bf16[2,1,32,256]{3,0,1,2:T(2,128)(2,1)S(1)} %copy.111), channel_id=9, replica_groups=mesh['lat'=16,'lon'=32] {'lon'}, use_global_device_ids=true, to_apply=%region_9.10.clone | all-reduce | flops 16384 | bytes 65536
  779.2 1.3 fusion.147
  780.4 1.2 fusion.146
  781.6 1.2 fusion.23
  782.8 1.2 fusion.24
  785.6 226.8 %all-reduce.9.cloned.1.call-done = f32[2,2,64,256]{3,2,1,0:T(8,128)} async-done(((f32[2,2,64,256]{3,2,1,0:T(8,128)}), f32[2,2,64,256]{3,2,1,0:T(8,128)}) %all-reduce.9.cloned.1.call-update) | async-done | bytes 262160
  1013.2 1.0 fusion.57
  1014.2 1.0 fusion.51
  1015.2 1.0 fusion.49
  1016.1 1.0 fusion.59
  1017.1 32.1 %all_gather.28 = f32[2,2,64,256]{3,1,0,2:T(2,128)S(1)} all-gather(f32[2,2,2,256]{3,1,0,2:T(2,128)S(1)} %pad_maximum_fusion.13), channel_id=1, replica_groups=mesh['lat'=16,'lon'=32] {'lon'}, dimensions={2}, use_global_device_ids=true | all-gather | bytes 270336 | tf_op jit(solution)/shard_map/all_gather | solution.py:142
  1051.2 32.3 %all_gather.30 = f32[2,1,32,256]{3,0,1,2:T(2,128)S(1)} all-gather(f32[2,1,1,256]{3,0,1,2:T(2,128)S(1)} %pad_maximum_fusion.15), channel_id=1, replica_groups=mesh['lat'=16,'lon'=32] {'lon'}, dimensions={2}, use_global_device_ids=true | all-gather | bytes 67584 | tf_op jit(solution)/shard_map/all_gather | solution.py:149
  1084.7 38.4 %all_gather.31 = f32[2,16,8,256]{3,2,1,0:T(8,128)S(1)} all-gather(f32[2,1,8,256]{3,2,1,0:T(8,128)S(1)} %pad_maximum_fusion.11), channel_id=1, replica_groups=mesh['lat'=16,'lon'=32] {'lat'}, dimensions={1}, use_global_device_ids=true | all-gather | bytes 278528 | tf_op jit(solution)/shard_map/all_gather | solution.py:151
  1124.2 1.3 slice_bitcast_fusion
  1125.5 1.0 fusion.83
  1126.6 1.1 fusion.19
  (133 shorter events, 27.2 us)
Async XLA Ops:
  7.2 560.0 %copy-start = (bf16[256,1024]{1,0:T(8,128)(2,1)S(1)}, bf16[256,1024]{1,0:T(8,128)(2,1)}, u32[]{:S(2)}) copy-start(bf16[256,1024]{1,0:T(8,128)(2,1)} %param.10) | copy-start | bytes 1572868
  7.2 3.6 copy-start.3
  7.2 99.6 %reduce-scatter.9.cloned.1.call-start = ((), (), s32[]{:S(2)}) async-start(), calls=%async_computation.6 | async-start | bytes 139264 | tf_op jit(solution)/shard_map/reduce_scatter | solution.py:121
  10.7 205.8 %reduce-scatter.7.cloned.1.call-start = ((), (), s32[]{:S(2)}) async-start(), calls=%async_computation.4 | async-start | bytes 1114112 | tf_op jit(solution)/shard_map/reduce_scatter | solution.py:108
  10.7 555.1 %copy-start.6 = (s32[32]{0:T(128)}, s32[32]{0:T(128)S(1)}, u32[]{:S(2)}) copy-start(s32[32]{0:T(128)S(1)} %get-tuple-element.31) | copy-start | bytes 388
  12.0 204.1 %copy-start.2 = (f32[1,1,2,256,256]{4,3,2,1,0:T(8,128)S(1)}, f32[1,1,2,256,256]{4,3,2,1,0:T(8,128)}, u32[]{:S(2)}) copy-start(f32[1,1,2,256,256]{4,3,2,1,0:T(8,128)} %param.9) | copy-start | bytes 1572868
  13.6 438.3 %copy-start.1 = (f32[2,2,2,256,256]{4,3,2,1,0:T(8,128)S(1)}, f32[2,2,2,256,256]{4,3,2,1,0:T(8,128)}, u32[]{:S(2)}) copy-start(f32[2,2,2,256,256]{4,3,2,1,0:T(8,128)} %param.8) | copy-start | bytes 6291460
  13.6 437.5 %all-reduce.7.cloned.1.call-start = ((), (), s32[]{:S(2)}) async-start(), calls=%async_computation.10 | async-start | bytes 524288
  15.9 505.8 %copy-start.8 = (s32[8]{0:T(128)}, s32[8]{0:T(128)S(1)}, u32[]{:S(2)}) copy-start(s32[8]{0:T(128)S(1)} %iota_add_fusion) | copy-start | bytes 100
  222.1 341.4 %all-gather.3.cloned.1.call-start = ((), (), s32[]{:S(2)}) async-start(), calls=%async_computation.5 | async-start | bytes 1114112 | tf_op jit(solution)/shard_map/all_gather | solution.py:144
  488.4 179.8 %reduce-scatter.13.cloned.1.call-start = ((), (), s32[]{:S(2)}) async-start(), calls=%async_computation.9 | async-start | bytes 139264 | tf_op jit(solution)/shard_map/reduce_scatter | solution.py:121
  563.5 2.3 copy-start.4
  567.1 1.8 copy-start.5
  578.6 200.6 %reduce-scatter.11.cloned.1.call-start = ((), (), s32[]{:S(2)}) async-start(), calls=%async_computation.7 | async-start | bytes 1114112 | tf_op jit(solution)/shard_map/reduce_scatter | solution.py:108
  582.5 85.6 %copy-start.9 = (s32[8]{0:T(128)S(1)}, s32[8]{0:T(128)}, u32[]{:S(2)}) copy-start(s32[8]{0:T(128)} %copy-done.8) | copy-start | bytes 100
  582.6 429.9 %all-reduce.9.cloned.1.call-start = ((), (), s32[]{:S(2)}) async-start(), calls=%async_computation.11 | async-start | bytes 524288
  784.8 339.5 %all-gather.5.cloned.1.call-start = ((), (), s32[]{:S(2)}) async-start(), calls=%async_computation.8 | async-start | bytes 1114112 | tf_op jit(solution)/shard_map/all_gather | solution.py:144
  1123.1 2.4 copy-start.7
Sparse Core Ops, SparseCore 0:
  12.6 94.1 reduce-scatter.8
  111.5 90.0 reduce-scatter.6
  222.2 228.8 all-reduce.6
  488.5 56.9 all-gather.2
  578.7 89.4 reduce-scatter.12
  672.1 89.8 reduce-scatter.10
  784.9 227.5 all-reduce.8
  1051.3 57.4 all-gather.4
where the time goes:
time: 1140 us
  waiting for transfers between devices  629 us (55%)
  blocking collectives  416 us (36%)
  matrix products  49.8 us (4%)
  between operations  15.5 us (1%)
  local copies, waits for them, and re-layouts  14.4 us (1%)
    unnamed x10, waiting for transfers between devices  456 us
    unnamed x2, blocking collectives  211 us
    reduce_scatter x2, waiting for transfers between devices, coarse_analysis(): lax.psum_scatter(lat_forward(grid_field, *tables[0]).astype(jnp.bfloat16)...  173 us
    all_gather x2, blocking collectives, coarse_synthesis(): lax.all_gather(mode_segment, 'lat', axis=1, tiled=True)  76.5 us
    all_gather x2, blocking collectives, coarse_synthesis(): gathered = lax.all_gather(spectrum, 'lon', axis=2, tiled=True)  64.7 us
    all_gather x2, blocking collectives, fine_synthesis(): gathered = lax.all_gather(spectrum, 'lon', axis=2, tiled=True)  64.3 us
  transfers between devices with their start and end apart: 8, of which 4 were waited for; matrix products, arithmetic and copies ran while one was open for 3% of the time, Pallas kernels for 0%

commit v1 on v0

v1 whole, which is shorter than its diff:
```python
from functools import partial
import math

import jax
import jax.numpy as jnp
import numpy as np
from jax import lax
from jax.experimental import pallas as pl
from jax.experimental.pallas import tpu as pltpu
from jax.sharding import PartitionSpec as P

f32 = jnp.float32
bf16 = jnp.bfloat16
MESH = pl.DeviceIdType.MESH
SLOTS = 8
PART = 16


def lon_table(lon_devices, columns):
    table = np.zeros((lon_devices, SLOTS, columns))
    w = np.arange(columns)
    for k in range(lon_devices):
        for b in range(2):
            angle = 2 * np.pi * ((2 * k + b) * w % columns) / columns
            table[k, 2 * b] = np.cos(angle)
            table[k, 2 * b + 1] = -np.sin(angle)
        angle = 2 * np.pi * (k * (w // 2) % (columns // 2)) / (columns // 2)
        table[k, 4] = np.cos(angle)
        table[k, 5] = -np.sin(angle)
    return table.reshape(lon_devices * SLOTS, columns)


def lat_tables(lat_devices, row_count):
    rows = lat_devices * row_count
    g = np.arange(rows).reshape(lat_devices, row_count)
    table = np.zeros((lat_devices, lat_devices, PART, row_count, SLOTS))
    for owner in range(lat_devices):
        for a in range(2):
            p = 2 * owner + a - lat_devices
            angle = 2 * np.pi * (p * g % rows) / rows
            for b in range(2):
                r = 4 * a + 2 * b
                table[:, owner, r, :, 2 * b] = np.cos(angle)
                table[:, owner, r, :, 2 * b + 1] = np.sin(angle)
                table[:, owner, r + 1, :, 2 * b] = -np.sin(angle)
                table[:, owner, r + 1, :, 2 * b + 1] = np.cos(angle)
        p = owner - lat_devices // 2
        angle = 2 * np.pi * (p * (g // 2) % (rows // 2)) / (rows // 2)
        table[:, owner, 8, :, 4] = np.cos(angle)
        table[:, owner, 8, :, 5] = np.sin(angle)
        table[:, owner, 9, :, 4] = -np.sin(angle)
        table[:, owner, 9, :, 5] = np.cos(angle)
    return table.reshape(lat_devices, lat_devices * PART, row_count * SLOTS)


def dot(a, b):
    return jnp.dot(a, b, preferred_element_type=f32)


def dot_t(a, b):
    return lax.dot_general(a, b, (((1,), (1,)), ((), ())), preferred_element_type=f32)


def split_halves(block):
    half = block.shape[1] // 2
    left = block[:, :half].reshape(-1, SLOTS, half)
    right = block[:, half:].reshape(-1, SLOTS, half)
    return jnp.concatenate([left, right], axis=1).astype(bf16)


def join_halves(messages):
    wide = messages.astype(f32)
    joined = jnp.concatenate([wide[:, :SLOTS], wide[:, SLOTS:]], axis=2)
    return joined.reshape(-1, joined.shape[2]).astype(bf16)


def gelu_parts(x):
    c = math.sqrt(2.0 / math.pi)
    square = x * x
    t = jnp.tanh(x * (c + (c * 0.044715) * square))
    half = 0.5 + 0.5 * t
    slope = half + (0.5 * x) * (1.0 - t * t) * (c + (3.0 * c * 0.044715) * square)
    return x * half, slope


def kernel(
    lat_devices, lon_devices, scale, tile,
    x_in, cot_in, fine_in, coarse_in, w_in_in, w_out_in, t_in, tt_in, l_in, lt_in,
    out_ref, grad_ref,
    fine32, coarse32, fine16, coarse16, w_in, w_out, t, tt, l, lt,
    xt, ct, s2, r2, s3, r3, s4, r4, s5, r5, d_act, act, mixed, d_mixed, out_rows, grad_rows,
    load_sem, own_sem, send_lon, recv_lon, send_lat, recv_lat,
):
    i = lax.axis_index("lat")
    k = lax.axis_index("lon")
    columns = lon_devices * 16
    channels = xt.shape[2]

    loads = [
        pltpu.make_async_copy(src, dst, load_sem.at[n])
        for n, (src, dst) in enumerate([
            (t_in, t), (tt_in, tt), (l_in.at[i], l), (lt_in.at[i], lt),
            (fine_in, fine32), (coarse_in, coarse32), (w_in_in, w_in), (w_out_in, w_out),
            (x_in.at[k], xt.at[k]), (cot_in.at[k], ct.at[k]),
        ])
    ]
    for load in loads:
        load.start()

    barrier = pltpu.get_barrier_semaphore()

    def greet_lon(d, _):
        pl.semaphore_signal(
            barrier, inc=1, device_id={"lon": lax.rem(k + d, lon_devices)}, device_id_type=MESH)
        return 0

    def greet_lat(d, _):
        pl.semaphore_signal(
            barrier, inc=1, device_id={"lat": lax.rem(i + d, lat_devices)}, device_id_type=MESH)
        return 0

    lax.fori_loop(1, lon_devices, greet_lon, 0)
    lax.fori_loop(1, lat_devices, greet_lat, 0)
    pl.semaphore_wait(barrier, lon_devices + lat_devices - 2)

    def send_to_lon(stage, source, target):
        def step(d, _):
            other = lax.rem(k + d, lon_devices)
            pltpu.make_async_remote_copy(
                src_ref=source.at[other], dst_ref=target.at[k],
                send_sem=send_lon.at[stage], recv_sem=recv_lon.at[stage],
                device_id={"lon": other}, device_id_type=MESH).start()
            return 0
        lax.fori_loop(1, lon_devices, step, 0)

    def send_to_lat(stage, source, target):
        def step(d, _):
            other = lax.rem(i + d, lat_devices)
            pltpu.make_async_remote_copy(
                src_ref=source.at[other], dst_ref=target.at[i],
                send_sem=send_lat.at[stage], recv_sem=recv_lat.at[stage],
                device_id={"lat": other}, device_id_type=MESH).start()
            return 0
        lax.fori_loop(1, lat_devices, step, 0)

    def spread_to_lat(stage, source, target):
        def step(d, _):
            other = lax.rem(i + d, lat_devices)
            pltpu.make_async_remote_copy(
                src_ref=source, dst_ref=target.at[i],
                send_sem=send_lat.at[stage], recv_sem=recv_lat.at[stage],
                device_id={"lat": other}, device_id_type=MESH).start()
            return 0
        lax.fori_loop(1, lat_devices, step, 0)

    def wait_all(buffer, sem):
        view = buffer.at[pl.ds(0, buffer.shape[0] - 1)]
        pltpu.make_async_copy(view, view, sem).wait()

    send_to_lon(0, x_in, xt)

    for n in range(4):
        loads[n].wait()
    for n in range(4, 8):
        loads[n].wait()
    fine16[...] = fine32[...].astype(bf16)
    coarse16[...] = coarse32[...].astype(bf16)

    def analysis(rows, way):
        s2[way] = split_halves(dot(t[...], rows))
        send_to_lon(1 + 4 * way, s2.at[way], r2.at[way])
        r2[way, k] = s2[way, k]

    def lat_analysis(way):
        wait_all(r2.at[way], recv_lon.at[1 + 4 * way])
        s3[way] = dot(l[...], join_halves(r2[way])).reshape(
            lat_devices, PART, channels).astype(bf16)
        send_to_lat(2 * way, s3.at[way], r3.at[way])
        r3[way, i] = s3[way, i]

    def spectrum(way):
        wait_all(r3.at[way], recv_lat.at[2 * way])
        return r3[way].astype(f32).sum(axis=0) * scale

    def turned(x):
        row = lax.broadcasted_iota(jnp.int32, x.shape, 0)
        up = jnp.concatenate([x[1:], x[:1]], axis=0)
        down = jnp.concatenate([x[-1:], x[:-1]], axis=0)
        return jnp.where(row % 2 == 0, -up, down)

    def mix(x, way):
        y = turned(x)
        x16 = x.astype(bf16)
        y16 = y.astype(bf16)
        row = lax.broadcasted_iota(jnp.int32, x.shape, 0)
        total = jnp.zeros_like(x)
        for m in range(5):
            if m < 4:
                w0 = fine16[m // 2, m % 2, 0]
                w1 = fine16[m // 2, m % 2, 1]
            else:
                w0 = coarse16[0, 0, 0]
                w1 = coarse16[0, 0, 1]
            if way == 0:
                mode = dot(x16, w0) + dot(y16, w1)
            else:
                mode = dot_t(x16, w0) - dot_t(y16, w1)
            total = jnp.where(row // 2 == m, mode, total)
        return total

    def spread(y, way):
        s4[way] = y.astype(bf16)
        spread_to_lat(2 * way + 1, s4.at[way], r4.at[way])
        r4[way, i] = s4[way]

    def lat_synthesis(way):
        wait_all(r4.at[way], recv_lat.at[2 * way + 1])
        s5[way] = split_halves(dot(lt[...], r4[way].reshape(lat_devices * PART, channels)))
        send_to_lon(3 + 3 * way, s5.at[way], r5.at[way])
        r5[way, k] = s5[way, k]

    loads[8].wait()
    wait_all(xt, recv_lon.at[0])
    analysis(xt[...].reshape(columns, channels), 0)
    send_to_lon(2, cot_in, ct)
    lat_analysis(0)
    spread(mix(spectrum(0), 0), 0)

    loads[9].wait()
    wait_all(ct, recv_lon.at[2])
    blocks = tile // 16
    for n in range(columns // tile):
        rows = pl.ds(n * tile, tile)
        cot = ct[pl.ds(n * blocks, blocks)].reshape(tile, channels)
        d_act[rows] = dot_t(cot, w_out[...])

    lat_synthesis(0)
    wait_all(r5.at[0], recv_lon.at[3])
    modes = join_halves(r5[0])
    for n in range(columns // tile):
        rows = pl.ds(n * tile, tile)
        part = pl.ds(n * blocks, blocks)
        x = xt[part].reshape(tile, channels).astype(f32)
        m = (x + dot(tt[rows], modes)).astype(bf16)
        mixed[rows] = m
        value, slope = gelu_parts(dot(m, w_in[...]))
        act[rows] = value.astype(bf16)
        d_hidden = (d_act[rows] * slope).astype(bf16)
        cot = ct[part].reshape(tile, channels).astype(f32)
        d_mixed[rows] = (cot + dot_t(d_hidden, w_in[...])).astype(bf16)

    analysis(d_mixed[...], 1)
    for n in range(columns // tile):
        rows = pl.ds(n * tile, tile)
        value = (mixed[rows].astype(f32) + dot(act[rows], w_out[...])).astype(bf16)
        out_rows[pl.ds(n * blocks, blocks)] = value.reshape(blocks, 16, channels)
    send_to_lon(4, out_rows, out_ref)
    own_out = pltpu.make_async_copy(out_rows.at[k], out_ref.at[k], own_sem.at[0])
    own_out.start()

    lat_analysis(1)
    spread(mix(spectrum(1), 1), 1)
    lat_synthesis(1)
    wait_all(r5.at[1], recv_lon.at[6])
    modes = join_halves(r5[1])
    for n in range(columns // tile):
        rows = pl.ds(n * tile, tile)
        value = (d_mixed[rows].astype(f32) + dot(tt[rows], modes)).astype(bf16)
        grad_rows[pl.ds(n * blocks, blocks)] = value.reshape(blocks, 16, channels)
    send_to_lon(7, grad_rows, grad_ref)
    own_grad = pltpu.make_async_copy(grad_rows.at[k], grad_ref.at[k], own_sem.at[1])
    own_grad.start()

    for stage, buffer in enumerate([
        xt, s2.at[0], ct, s5.at[0], out_rows, s2.at[1], s5.at[1], grad_rows,
    ]):
        wait_all(buffer, send_lon.at[stage])
    for stage, buffer in enumerate([r3.at[0], r4.at[0], r3.at[1], r4.at[1]]):
        wait_all(buffer, send_lat.at[stage])
    wait_all(out_ref, recv_lon.at[4])
    wait_all(grad_ref, recv_lon.at[7])
    own_out.wait()
    own_grad.wait()


def local(t, tt, l, lt, inputs, cotangent, spectral_fine, spectral_coarse, weight_in, weight_out):
    row_count, column_count, channels = inputs.shape
    hidden = weight_in.shape[1]
    lat_devices = lax.axis_size("lat")
    lon_devices = lax.axis_size("lon")
    columns = column_count * lon_devices
    rows = row_count * lat_devices
    assert row_count == lon_devices and column_count == 16
    scale = 1.0 / math.sqrt(rows * columns * 4 * lat_devices * lon_devices)
    tile = min(128, columns)
    half = channels // 2
    lon_message = (2, lon_devices, 2 * SLOTS, half)
    lat_message = (2, lat_devices, PART, channels)
    field = (lon_devices, column_count, channels)
    shape = jax.ShapeDtypeStruct((row_count, column_count, channels), bf16)
    anywhere = pl.BlockSpec(memory_space=pl.ANY)
    scratch = [
        (spectral_fine.shape, f32), (spectral_coarse.shape, f32),
        (spectral_fine.shape, bf16), (spectral_coarse.shape, bf16),
        (weight_in.shape, bf16), (weight_out.shape, bf16),
        (t.shape, bf16), (tt.shape, bf16), (l.shape[1:], bf16), (lt.shape[1:], bf16),
        (field, bf16), (field, bf16),
        (lon_message, bf16), (lon_message, bf16),
        (lat_message, bf16), (lat_message, bf16),
        ((2, PART, channels), bf16), (lat_message, bf16),
        (lon_message, bf16), (lon_message, bf16),
        ((columns, hidden), f32), ((columns, hidden), bf16),
        ((columns, channels), bf16), ((columns, channels), bf16),
        (field, bf16), (field, bf16),
    ]
    return pl.pallas_call(
        partial(kernel, lat_devices, lon_devices, scale, tile),
        out_shape=(shape, shape),
        in_specs=[anywhere] * 10,
        out_specs=(anywhere, anywhere),
        scratch_shapes=[pltpu.VMEM(dims, kind) for dims, kind in scratch] + [
            pltpu.SemaphoreType.DMA((10,)),
            pltpu.SemaphoreType.DMA((2,)),
            pltpu.SemaphoreType.DMA((8,)),
            pltpu.SemaphoreType.DMA((8,)),
            pltpu.SemaphoreType.DMA((4,)),
            pltpu.SemaphoreType.DMA((4,)),
        ],
        compiler_params=pltpu.CompilerParams(
            collective_id=0, has_side_effects=True, vmem_limit_bytes=40 * 1024 * 1024),
    )(inputs, cotangent, spectral_fine, spectral_coarse, weight_in, weight_out, t, tt, l, lt)


def solution(mesh):
    lat_devices, lon_devices = mesh.shape["lat"], mesh.shape["lon"]
    t = lon_table(lon_devices, 16 * lon_devices)
    l = lat_tables(lat_devices, lon_devices)
    tables = [
        np.asarray(table).astype(jnp.bfloat16)
        for table in (t, t.T, l, np.swapaxes(l, 1, 2))
    ]
    field = P("lat", "lon", None)
    modes = P("lat", "lon", None, None, None)
    body = jax.shard_map(
        local,
        mesh=mesh,
        in_specs=(P(), P(), P(), P(), field, field, modes, modes, P(), P()),
        out_specs=(field, field),
        check_vma=False,
    )

    def run(inputs, cotangent, spectral_fine, spectral_coarse, weight_in, weight_out):
        return body(
            *(jnp.asarray(table) for table in tables),
            inputs, cotangent, spectral_fine, spectral_coarse, weight_in, weight_out)

    return run
```

time: 1140 us -> 112 us (0.10)
  waiting for transfers between devices: 629 us -> 0 us
  blocking collectives: 416 us -> 0 us
  Pallas kernels: 0 us -> 97.4 us
  matrix products: 49.8 us -> 0 us
  between operations: 15.5 us -> 0.66 us
    unnamed x10 -> x0, waiting for transfers between devices: 456 us -> none
    unnamed x2 -> x0, blocking collectives: 211 us -> none
    all_gather x6 -> x0, blocking collectives: 205 us -> none  [the longest x2 76.5 us: coarse_synthesis(): lax.all_gather(mode_segment, 'lat', axis=1, tiled=True)]
    reduce_scatter x4 -> x0, waiting for transfers between devices: 173 us -> none  [the longest x2 173 us: coarse_analysis(): lax.psum_scatter(lat_forward(grid_field, *tables[0]).astype(jnp.bfloat16)...]
    pallas_call x0 -> x1, Pallas kernels: none -> 97.4 us  [local(): pl.pallas_call(partial(kernel, lat_devices, lon_devices, scale, tile), ou...]
    dot_general x67 -> x0, matrix products: 49.8 us -> none  [the longest x4 4.28 us: lon_forward(): jnp.einsum('kw,jwc->jkc', cos_lon, mode_segment[1], precision=highest)]
  transfers between devices with their start and end apart: 8 -> 0, of which waited for: 4 -> 0; matrix products, arithmetic and copies ran while one was open for 3% -> 0% of each run, Pallas kernels for 0% -> 0%
where the time goes in v1:
time: 112 us; the launch traced here: 111 us
  Pallas kernels  97.4 us (87%)
  local copies, waits for them, and re-layouts  13.1 us (12%)
    pallas_call x1, Pallas kernels, local(): pl.pallas_call(partial(kernel, lat_devices, lon_devices, scale, tile), ou...  97.4 us
    unnamed x22, local copies, waits for them, and re-layouts  13.1 us

profile of v1, /device:TPU:1, one launch (start us, length us, event | category | flops | bytes accessed | tf_op | source)
XLA Modules:
  0.0 111.1 jit_solution(14282584582786437061)
XLA Ops:
  0.6 0.0 copy-start
  0.6 1.6 %copy-done = f32[2,2,2,256,256]{4,3,2,1,0:T(8,128)S(1)} copy-done((f32[2,2,2,256,256]{4,3,2,1,0:T(8,128)S(1)}, f32[2,2,2,256,256]{4,3,2,1,0:T(8,128)}, u32[]{:S(2)}) %copy-start) | copy-done | bytes 2097176
  2.2 0.0 copy-start.1
  2.2 1.6 %copy-done.1 = bf16[16,256,256]{2,1,0:T(8,128)(2,1)S(1)} copy-done((bf16[16,256,256]{2,1,0:T(8,128)(2,1)S(1)}, bf16[16,256,256]{2,1,0:T(8,128)(2,1)}, u32[]{:S(2)}) %copy-start.1) | copy-done | bytes 2097176
  3.8 0.0 copy-start.2
  3.8 1.6 %copy-done.2 = bf16[16,256,256]{2,1,0:T(8,128)(2,1)S(1)} copy-done((bf16[16,256,256]{2,1,0:T(8,128)(2,1)S(1)}, bf16[16,256,256]{2,1,0:T(8,128)(2,1)}, u32[]{:S(2)}) %copy-start.2) | copy-done | bytes 2097176
  5.4 0.0 copy-start.3
  5.4 1.0 copy-done.3
  6.4 0.0 copy-start.4
  6.5 1.0 copy-done.4
  7.5 0.0 copy-start.5
  7.5 1.0 copy-done.5
  8.5 0.0 copy-start.6
  8.5 0.9 copy-done.6
  9.5 0.0 copy-start.7
  9.5 0.9 copy-done.7
  10.4 0.0 copy-start.8
  10.4 0.9 copy-done.8
  11.4 0.0 copy-start.9
  11.4 0.9 copy-done.9
  12.3 97.4 %shard_map.113 = (bf16[32,16,256]{2,1,0:T(8,128)(2,1)S(1)}, bf16[32,16,256]{2,1,0:T(8,128)(2,1)S(1)}) custom-call(bf16[32,16,256]{2,1,0:T(8,128)(2,1)S(1)} %copy-done.6, bf16[32,16,256]{2,1,0:T(8,128)(2,1)S(1)} %copy-done.7, f32[2,2,2,256,256]{4,3,2,1,0:T(8,128)S(1)} %copy-done, f32[1,1,2,256,256]{4,3,2,1,0:T(8,128)S(1)} %copy-done.3, ...), custom_call_target="tpu_custom_call" | custom-call | tf_op jit(solution)/shard_map/pallas_call | solution.py:316
  109.7 0.7 copy.14
  110.4 0.7 copy.15
Async XLA Ops:
  0.6 1.6 %copy-start = (f32[2,2,2,256,256]{4,3,2,1,0:T(8,128)S(1)}, f32[2,2,2,256,256]{4,3,2,1,0:T(8,128)}, u32[]{:S(2)}) copy-start(f32[2,2,2,256,256]{4,3,2,1,0:T(8,128)} %fine_in.1) | copy-start | bytes 6291460
  2.2 1.6 %copy-start.1 = (bf16[16,256,256]{2,1,0:T(8,128)(2,1)S(1)}, bf16[16,256,256]{2,1,0:T(8,128)(2,1)}, u32[]{:S(2)}) copy-start(bf16[16,256,256]{2,1,0:T(8,128)(2,1)} %constant.11.clone.lt_in) | copy-start | bytes 6291460
  3.8 1.6 %copy-start.2 = (bf16[16,256,256]{2,1,0:T(8,128)(2,1)S(1)}, bf16[16,256,256]{2,1,0:T(8,128)(2,1)}, u32[]{:S(2)}) copy-start(bf16[16,256,256]{2,1,0:T(8,128)(2,1)} %constant.10.clone.l_in) | copy-start | bytes 6291460
  5.4 1.0 copy-start.3
  6.4 1.0 copy-start.4
  7.5 1.0 copy-start.5
  8.5 0.9 copy-start.6
  9.5 0.9 copy-start.7
  10.4 0.9 copy-start.8
  11.4 0.9 copy-start.9

commit v2 on v1

--- a/solution.py
+++ b/solution.py
@@ -14,7 +14,6 @@
 MESH = pl.DeviceIdType.MESH
 SLOTS = 8
 PART = 16
-
 
 def lon_table(lon_devices, columns):
     table = np.zeros((lon_devices, SLOTS, columns))
@@ -28,7 +27,6 @@
         table[k, 4] = np.cos(angle)
         table[k, 5] = -np.sin(angle)
     return table.reshape(lon_devices * SLOTS, columns)
-
 
 def lat_tables(lat_devices, row_count):
     rows = lat_devices * row_count
@@ -52,14 +50,11 @@
         table[:, owner, 9, :, 5] = np.cos(angle)
     return table.reshape(lat_devices, lat_devices * PART, row_count * SLOTS)
 
-
 def dot(a, b):
     return jnp.dot(a, b, preferred_element_type=f32)
 
-
 def dot_t(a, b):
     return lax.dot_general(a, b, (((1,), (1,)), ((), ())), preferred_element_type=f32)
-
 
 def split_halves(block):
     half = block.shape[1] // 2
@@ -67,12 +62,10 @@
     right = block[:, half:].reshape(-1, SLOTS, half)
     return jnp.concatenate([left, right], axis=1).astype(bf16)
 
-
 def join_halves(messages):
     wide = messages.astype(f32)
     joined = jnp.concatenate([wide[:, :SLOTS], wide[:, SLOTS:]], axis=2)
     return joined.reshape(-1, joined.shape[2]).astype(bf16)
-
 
 def gelu_parts(x):
     c = math.sqrt(2.0 / math.pi)
@@ -82,13 +75,12 @@
     slope = half + (0.5 * x) * (1.0 - t * t) * (c + (3.0 * c * 0.044715) * square)
     return x * half, slope
 
-
 def kernel(
     lat_devices, lon_devices, scale, tile,
     x_in, cot_in, fine_in, coarse_in, w_in_in, w_out_in, t_in, tt_in, l_in, lt_in,
     out_ref, grad_ref,
     fine32, coarse32, fine16, coarse16, w_in, w_out, t, tt, l, lt,
-    xt, ct, s2, r2, s3, r3, s4, r4, s5, r5, d_act, act, mixed, d_mixed, out_rows, grad_rows,
+    xt, ct, s2, r2, s3, r3, s4, r4, s5, r5, d_act, act, mixed, d_mixed, out_rows, grad_rows, x_own, cot_own,
     load_sem, own_sem, send_lon, recv_lon, send_lat, recv_lat,
 ):
     i = lax.axis_index("lat")
@@ -99,72 +91,96 @@
     loads = [
         pltpu.make_async_copy(src, dst, load_sem.at[n])
         for n, (src, dst) in enumerate([
-            (t_in, t), (tt_in, tt), (l_in.at[i], l), (lt_in.at[i], lt),
-            (fine_in, fine32), (coarse_in, coarse32), (w_in_in, w_in), (w_out_in, w_out),
-            (x_in.at[k], xt.at[k]), (cot_in.at[k], ct.at[k]),
+            (x_in, x_own), (t_in, t), (l_in.at[i], l), (fine_in, fine32), (coarse_in, coarse32),
+            (cot_in, cot_own), (lt_in.at[i], lt), (w_out_in, w_out), (tt_in, tt), (w_in_in, w_in),
         ])
     ]
     for load in loads:
         load.start()
 
+    def centre_out(j, n):
+        return n // 2 + (j + 1) // 2 * (1 - 2 * (j % 2))
+
+    def lon_partner(j):
+        inner = min(4, lon_devices)
+        outer = lon_devices // inner
+        z = (k // inner + centre_out(j // inner, outer)) % outer
+        return z * inner + (k + inner - 1 - j % inner) % inner
+
+    def lat_partner(j):
+        inner = min(4, lat_devices)
+        outer = lat_devices // inner
+        x = (i // inner + centre_out(j % outer, outer)) % outer
+        return x * inner + (i + centre_out(j // outer, inner)) % inner
+
     barrier = pltpu.get_barrier_semaphore()
 
-    def greet_lon(d, _):
+    def greet_lat(j, _):
         pl.semaphore_signal(
-            barrier, inc=1, device_id={"lon": lax.rem(k + d, lon_devices)}, device_id_type=MESH)
+            barrier, inc=1, device_id={"lat": lat_partner(j)}, device_id_type=MESH)
         return 0
 
-    def greet_lat(d, _):
+    def greet_lon(j, _):
         pl.semaphore_signal(
-            barrier, inc=1, device_id={"lat": lax.rem(i + d, lat_devices)}, device_id_type=MESH)
+            barrier, inc=1, device_id={"lon": lon_partner(j)}, device_id_type=MESH)
         return 0
 
-    lax.fori_loop(1, lon_devices, greet_lon, 0)
-    lax.fori_loop(1, lat_devices, greet_lat, 0)
+    lax.fori_loop(0, lat_devices - 1, greet_lat, 0)
+    lax.fori_loop(0, lon_devices - 1, greet_lon, 0)
     pl.semaphore_wait(barrier, lon_devices + lat_devices - 2)
 
+    pending = []
+    arriving = {}
+
     def send_to_lon(stage, source, target):
-        def step(d, _):
-            other = lax.rem(k + d, lon_devices)
+        pending.append((target, send_lon.at[stage]))
+        arriving['lon', stage] = (target, recv_lon.at[stage])
+
+        def step(j, _):
+            other = lon_partner(j)
             pltpu.make_async_remote_copy(
                 src_ref=source.at[other], dst_ref=target.at[k],
                 send_sem=send_lon.at[stage], recv_sem=recv_lon.at[stage],
                 device_id={"lon": other}, device_id_type=MESH).start()
             return 0
-        lax.fori_loop(1, lon_devices, step, 0)
-
-    def send_to_lat(stage, source, target):
-        def step(d, _):
-            other = lax.rem(i + d, lat_devices)
+        lax.fori_loop(0, lon_devices - 1, step, 0)
+
+    def send_to_lat(stage, source, target, spread=False):
+        pending.append((target, send_lat.at[stage]))
+        arriving['lat', stage] = (target, recv_lat.at[stage])
+
+        def step(j, _):
+            other = lat_partner(j)
             pltpu.make_async_remote_copy(
-                src_ref=source.at[other], dst_ref=target.at[i],
+                src_ref=source if spread else source.at[other], dst_ref=target.at[i],
                 send_sem=send_lat.at[stage], recv_sem=recv_lat.at[stage],
                 device_id={"lat": other}, device_id_type=MESH).start()
             return 0
-        lax.fori_loop(1, lat_devices, step, 0)
-
-    def spread_to_lat(stage, source, target):
-        def step(d, _):
-            other = lax.rem(i + d, lat_devices)
-            pltpu.make_async_remote_copy(
-                src_ref=source, dst_ref=target.at[i],
-                send_sem=send_lat.at[stage], recv_sem=recv_lat.at[stage],
-                device_id={"lat": other}, device_id_type=MESH).start()
-            return 0
-        lax.fori_loop(1, lat_devices, step, 0)
+        lax.fori_loop(0, lat_devices - 1, step, 0)
+
+    def arrive(group, stage):
+        wait_all(*arriving.pop((group, stage)))
 
     def wait_all(buffer, sem):
         view = buffer.at[pl.ds(0, buffer.shape[0] - 1)]
         pltpu.make_async_copy(view, view, sem).wait()
 
-    send_to_lon(0, x_in, xt)
-
-    for n in range(4):
-        loads[n].wait()
-    for n in range(4, 8):
-        loads[n].wait()
-    fine16[...] = fine32[...].astype(bf16)
-    coarse16[...] = coarse32[...].astype(bf16)
+    opened = dict(enumerate(loads))
+
+    def ready(n):
+        opened.pop(n).wait()
+
+    def end():
+        for buffer, sem in pending:
+            wait_all(buffer, sem)
+        for buffer, sem in arriving.values():
+            wait_all(buffer, sem)
+        for load in opened.values():
+            load.wait()
+
+    ready(0)
+    send_to_lon(0, x_own, xt)
+    xt[k] = x_own[k]
 
     def analysis(rows, way):
         s2[way] = split_halves(dot(t[...], rows))
@@ -172,14 +188,14 @@
         r2[way, k] = s2[way, k]
 
     def lat_analysis(way):
-        wait_all(r2.at[way], recv_lon.at[1 + 4 * way])
+        arrive('lon', 1 + 4 * way)
         s3[way] = dot(l[...], join_halves(r2[way])).reshape(
             lat_devices, PART, channels).astype(bf16)
         send_to_lat(2 * way, s3.at[way], r3.at[way])
         r3[way, i] = s3[way, i]
 
     def spectrum(way):
-        wait_all(r3.at[way], recv_lat.at[2 * way])
+        arrive('lat', 2 * way)
         return r3[way].astype(f32).sum(axis=0) * scale
 
     def turned(x):
@@ -210,24 +226,34 @@
 
     def spread(y, way):
         s4[way] = y.astype(bf16)
-        spread_to_lat(2 * way + 1, s4.at[way], r4.at[way])
+        send_to_lat(2 * way + 1, s4.at[way], r4.at[way], spread=True)
         r4[way, i] = s4[way]
 
     def lat_synthesis(way):
-        wait_all(r4.at[way], recv_lat.at[2 * way + 1])
+        arrive('lat', 2 * way + 1)
         s5[way] = split_halves(dot(lt[...], r4[way].reshape(lat_devices * PART, channels)))
         send_to_lon(3 + 3 * way, s5.at[way], r5.at[way])
         r5[way, k] = s5[way, k]
 
-    loads[8].wait()
-    wait_all(xt, recv_lon.at[0])
+    arrive('lon', 0)
+
+    ready(1)
     analysis(xt[...].reshape(columns, channels), 0)
-    send_to_lon(2, cot_in, ct)
+    for n in (2, 3, 4):
+        ready(n)
+    fine16[...] = fine32[...].astype(bf16)
+    coarse16[...] = coarse32[...].astype(bf16)
+
     lat_analysis(0)
+
+    ready(5)
+    send_to_lon(2, cot_own, ct)
+    ct[k] = cot_own[k]
     spread(mix(spectrum(0), 0), 0)
 
-    loads[9].wait()
-    wait_all(ct, recv_lon.at[2])
+    for n in (6, 7, 8, 9):
+        ready(n)
+    arrive('lon', 2)
     blocks = tile // 16
     for n in range(columns // tile):
         rows = pl.ds(n * tile, tile)
@@ -235,7 +261,8 @@
         d_act[rows] = dot_t(cot, w_out[...])
 
     lat_synthesis(0)
-    wait_all(r5.at[0], recv_lon.at[3])
+
+    arrive('lon', 3)
     modes = join_halves(r5[0])
     for n in range(columns // tile):
         rows = pl.ds(n * tile, tile)
@@ -257,31 +284,42 @@
     send_to_lon(4, out_rows, out_ref)
     own_out = pltpu.make_async_copy(out_rows.at[k], out_ref.at[k], own_sem.at[0])
     own_out.start()
+    opened['out'] = own_out
 
     lat_analysis(1)
+
     spread(mix(spectrum(1), 1), 1)
+
     lat_synthesis(1)
-    wait_all(r5.at[1], recv_lon.at[6])
+
+    arrive('lon', 6)
     modes = join_halves(r5[1])
     for n in range(columns // tile):
         rows = pl.ds(n * tile, tile)
         value = (d_mixed[rows].astype(f32) + dot(tt[rows], modes)).astype(bf16)
         grad_rows[pl.ds(n * blocks, blocks)] = value.reshape(blocks, 16, channels)
+
     send_to_lon(7, grad_rows, grad_ref)
     own_grad = pltpu.make_async_copy(grad_rows.at[k], grad_ref.at[k], own_sem.at[1])
     own_grad.start()
-
-    for stage, buffer in enumerate([
-        xt, s2.at[0], ct, s5.at[0], out_rows, s2.at[1], s5.at[1], grad_rows,
-    ]):
-        wait_all(buffer, send_lon.at[stage])
-    for stage, buffer in enumerate([r3.at[0], r4.at[0], r3.at[1], r4.at[1]]):
-        wait_all(buffer, send_lat.at[stage])
-    wait_all(out_ref, recv_lon.at[4])
-    wait_all(grad_ref, recv_lon.at[7])
-    own_out.wait()
-    own_grad.wait()
-
+    opened['grad'] = own_grad
+
+    end()
+
+def hand_over(a_in, b_in, a_out, b_out, held, sem):
+    arrive = [
+        pltpu.make_async_copy(src, held.at[n], sem.at[n]) for n, src in enumerate((a_in, b_in))
+    ]
+    leave = [
+        pltpu.make_async_copy(held.at[n], dst, sem.at[2 + n]) for n, dst in enumerate((a_out, b_out))
+    ]
+    for copy in arrive:
+        copy.start()
+    for n in range(2):
+        arrive[n].wait()
+        leave[n].start()
+    for copy in leave:
+        copy.wait()
 
 def local(t, tt, l, lt, inputs, cotangent, spectral_fine, spectral_coarse, weight_in, weight_out):
     row_count, column_count, channels = inputs.shape
@@ -298,7 +336,7 @@
     lat_message = (2, lat_devices, PART, channels)
     field = (lon_devices, column_count, channels)
     shape = jax.ShapeDtypeStruct((row_count, column_count, channels), bf16)
-    anywhere = pl.BlockSpec(memory_space=pl.ANY)
+    anywhere = pl.BlockSpec(memory_space=pltpu.HBM)
     scratch = [
         (spectral_fine.shape, f32), (spectral_coarse.shape, f32),
         (spectral_fine.shape, bf16), (spectral_coarse.shape, bf16),
@@ -311,9 +349,9 @@
         (lon_message, bf16), (lon_message, bf16),
         ((columns, hidden), f32), ((columns, hidden), bf16),
         ((columns, channels), bf16), ((columns, channels), bf16),
-        (field, bf16), (field, bf16),
+        (field, bf16), (field, bf16), (field, bf16), (field, bf16),
     ]
-    return pl.pallas_call(
+    results = pl.pallas_call(
         partial(kernel, lat_devices, lon_devices, scale, tile),
         out_shape=(shape, shape),
         in_specs=[anywhere] * 10,
@@ -327,9 +365,16 @@
             pltpu.SemaphoreType.DMA((4,)),
         ],
         compiler_params=pltpu.CompilerParams(
-            collective_id=0, has_side_effects=True, vmem_limit_bytes=40 * 1024 * 1024),
+            collective_id=0, has_side_effects=True, vmem_limit_bytes=56 * 1024 * 1024),
     )(inputs, cotangent, spectral_fine, spectral_coarse, weight_in, weight_out, t, tt, l, lt)
-
+    return pl.pallas_call(
+        hand_over,
+        out_shape=(shape, shape),
+        in_specs=[anywhere] * 2,
+        out_specs=(anywhere, anywhere),
+        scratch_shapes=[pltpu.VMEM((2,) + shape.shape, bf16), pltpu.SemaphoreType.DMA((4,))],
+        compiler_params=pltpu.CompilerParams(vmem_limit_bytes=56 * 1024 * 1024),
+    )(*results)
 
 def solution(mesh):
     lat_devices, lon_devices = mesh.shape["lat"], mesh.shape["lon"]

time: 112 us -> 91.5 us (0.82)
  local copies, waits for them, and re-layouts: 13.1 us -> 0 us
  Pallas kernels: 97.4 us -> 90.7 us
    unnamed x22 -> x0, local copies, waits for them, and re-layouts: 13.1 us -> none
    pallas_call x1, Pallas kernels: 97.4 us -> 89 us  [local(): pl.pallas_call(partial(kernel, lat_devices, lon_devices, scale, tile), ou...]
    pallas_call x0 -> x1, Pallas kernels: none -> 1.77 us  [local(): pl.pallas_call(hand_over, out_shape=(shape, shape), in_specs=[anywhere] *...]
where the time goes in v2:
time: 91.5 us; the launch traced here: 91.4 us
  Pallas kernels  90.7 us (99%)
    pallas_call x1, Pallas kernels, local(): pl.pallas_call(partial(kernel, lat_devices, lon_devices, scale, tile), ou...  89 us

profile of v2, /device:TPU:1, one launch (start us, length us, event | category | flops | bytes accessed | tf_op | source)
XLA Modules:
  0.0 91.4 jit_solution(4260718545171892395)
XLA Ops:
  0.6 89.0 %shard_map.113 = (bf16[32,16,256]{2,1,0:T(8,128)(2,1)}, bf16[32,16,256]{2,1,0:T(8,128)(2,1)}) custom-call(bf16[32,16,256]{2,1,0:T(8,128)(2,1)} %x_in.1, bf16[32,16,256]{2,1,0:T(8,128)(2,1)} %cot_in.1, f32[2,2,2,256,256]{4,3,2,1,0:T(8,128)} %fine_in.1, f32[1,1,2,256,256]{4,3,2,1,0:T(8,128)} %coarse_in.1, bf16[256,1024]{1,0:T(8,128)(2,1)} %w_in_in.1, ...), custom_call_target="tpu_custom_call" | custom-call | tf_op jit(solution)/shard_map/pallas_call | solution.py:354
  89.6 1.8 %shard_map.114 = (bf16[32,16,256]{2,1,0:T(8,128)(2,1)}, bf16[32,16,256]{2,1,0:T(8,128)(2,1)}) custom-call(bf16[32,16,256]{2,1,0:T(8,128)(2,1)} %get-tuple-element.4.a_in, bf16[32,16,256]{2,1,0:T(8,128)(2,1)} %get-tuple-element.5.b_in), custom_call_target="tpu_custom_call" | custom-call | tf_op jit(solution)/shard_map/pallas_call | solution.py:370

commit v3 on v2

--- a/solution.py
+++ b/solution.py
@@ -95,23 +95,25 @@
             (cot_in, cot_own), (lt_in.at[i], lt), (w_out_in, w_out), (tt_in, tt), (w_in_in, w_in),
         ])
     ]
-    for load in loads:
-        load.start()
+    loads[0].start()
 
     def centre_out(j, n):
-        return n // 2 + (j + 1) // 2 * (1 - 2 * (j % 2))
+        half = lax.div(j + 1, 2)
+        return n // 2 + jnp.where(lax.rem(j, 2) == 0, half, -half)
+
+    lon_inner = min(4, lon_devices)
+    lon_outer = lon_devices // lon_inner
+    lat_inner = min(4, lat_devices)
+    lat_outer = lat_devices // lat_inner
+    z_here, x_here = lax.div(k, lon_inner), lax.div(i, lat_inner)
 
     def lon_partner(j):
-        inner = min(4, lon_devices)
-        outer = lon_devices // inner
-        z = (k // inner + centre_out(j // inner, outer)) % outer
-        return z * inner + (k + inner - 1 - j % inner) % inner
+        to = lax.rem(z_here + centre_out(lax.div(j, lon_inner), lon_outer), lon_outer)
+        return to * lon_inner + lax.rem(k + (lon_inner - 1) - lax.rem(j, lon_inner), lon_inner)
 
     def lat_partner(j):
-        inner = min(4, lat_devices)
-        outer = lat_devices // inner
-        x = (i // inner + centre_out(j % outer, outer)) % outer
-        return x * inner + (i + centre_out(j // outer, inner)) % inner
+        to = lax.rem(x_here + centre_out(lax.rem(j, lat_outer), lat_outer), lat_outer)
+        return to * lat_inner + lax.rem(i + centre_out(lax.div(j, lat_outer), lat_inner), lat_inner)
 
     barrier = pltpu.get_barrier_semaphore()
 
@@ -127,6 +129,8 @@
 
     lax.fori_loop(0, lat_devices - 1, greet_lat, 0)
     lax.fori_loop(0, lon_devices - 1, greet_lon, 0)
+    for load in loads[1:]:
+        load.start()
     pl.semaphore_wait(barrier, lon_devices + lat_devices - 2)
 
     pending = []
@@ -281,12 +285,13 @@
         rows = pl.ds(n * tile, tile)
         value = (mixed[rows].astype(f32) + dot(act[rows], w_out[...])).astype(bf16)
         out_rows[pl.ds(n * blocks, blocks)] = value.reshape(blocks, 16, channels)
+
+    lat_analysis(1)
+
     send_to_lon(4, out_rows, out_ref)
     own_out = pltpu.make_async_copy(out_rows.at[k], out_ref.at[k], own_sem.at[0])
     own_out.start()
     opened['out'] = own_out
-
-    lat_analysis(1)
 
     spread(mix(spectrum(1), 1), 1)
 

time: 91.5 us -> 87.8 us (0.960)
  Pallas kernels: 90.7 us -> 87 us
    pallas_call x1, Pallas kernels: 89 us -> 85.2 us  [local(): pl.pallas_call(partial(kernel, lat_devices, lon_devices, scale, tile), ou...]
where the time goes in v3:
time: 87.8 us; the launch traced here: 87.7 us
  Pallas kernels  87 us (99%)
    pallas_call x1, Pallas kernels, local(): pl.pallas_call(partial(kernel, lat_devices, lon_devices, scale, tile), ou...  85.2 us
    pallas_call x1, Pallas kernels, local(): pl.pallas_call(hand_over, out_shape=(shape, shape), in_specs=[anywhere] *...  1.77 us

profile of v3, /device:TPU:1, one launch (start us, length us, event | category | flops | bytes accessed | tf_op | source)
XLA Modules:
  0.0 87.7 jit_solution(17960545316829839514)
XLA Ops:
  0.6 85.2 %shard_map.113 = (bf16[32,16,256]{2,1,0:T(8,128)(2,1)}, bf16[32,16,256]{2,1,0:T(8,128)(2,1)}) custom-call(bf16[32,16,256]{2,1,0:T(8,128)(2,1)} %x_in.1, bf16[32,16,256]{2,1,0:T(8,128)(2,1)} %cot_in.1, f32[2,2,2,256,256]{4,3,2,1,0:T(8,128)} %fine_in.1, f32[1,1,2,256,256]{4,3,2,1,0:T(8,128)} %coarse_in.1, bf16[256,1024]{1,0:T(8,128)(2,1)} %w_in_in.1, ...), custom_call_target="tpu_custom_call" | custom-call | tf_op jit(solution)/shard_map/pallas_call | solution.py:359
  85.9 1.8 %shard_map.114 = (bf16[32,16,256]{2,1,0:T(8,128)(2,1)}, bf16[32,16,256]{2,1,0:T(8,128)(2,1)}) custom-call(bf16[32,16,256]{2,1,0:T(8,128)(2,1)} %get-tuple-element.4.a_in, bf16[32,16,256]{2,1,0:T(8,128)(2,1)} %get-tuple-element.5.b_in), custom_call_target="tpu_custom_call" | custom-call | tf_op jit(solution)/shard_map/pallas_call | solution.py:375

commit v4 on v3

--- a/solution.py
+++ b/solution.py
@@ -311,18 +311,13 @@
 
     end()
 
-def hand_over(a_in, b_in, a_out, b_out, held, sem):
-    arrive = [
-        pltpu.make_async_copy(src, held.at[n], sem.at[n]) for n, src in enumerate((a_in, b_in))
+def hand_over(a_in, b_in, a_out, b_out, sem):
+    leave = [
+        pltpu.make_async_copy(src, dst, sem.at[n])
+        for n, (src, dst) in enumerate(((a_in, a_out), (b_in, b_out)))
     ]
-    leave = [
-        pltpu.make_async_copy(held.at[n], dst, sem.at[2 + n]) for n, dst in enumerate((a_out, b_out))
-    ]
-    for copy in arrive:
+    for copy in leave:
         copy.start()
-    for n in range(2):
-        arrive[n].wait()
-        leave[n].start()
     for copy in leave:
         copy.wait()
 
@@ -335,7 +330,7 @@
     rows = row_count * lat_devices
     assert row_count == lon_devices and column_count == 16
     scale = 1.0 / math.sqrt(rows * columns * 4 * lat_devices * lon_devices)
-    tile = min(128, columns)
+    tile = min(512, columns)
     half = channels // 2
     lon_message = (2, lon_devices, 2 * SLOTS, half)
     lat_message = (2, lat_devices, PART, channels)
@@ -358,9 +353,9 @@
     ]
     results = pl.pallas_call(
         partial(kernel, lat_devices, lon_devices, scale, tile),
-        out_shape=(shape, shape),
+        out_shape=(pltpu.VMEM(shape.shape, bf16), pltpu.VMEM(shape.shape, bf16)),
         in_specs=[anywhere] * 10,
-        out_specs=(anywhere, anywhere),
+        out_specs=(pl.BlockSpec(memory_space=pl.ANY),) * 2,
         scratch_shapes=[pltpu.VMEM(dims, kind) for dims, kind in scratch] + [
             pltpu.SemaphoreType.DMA((10,)),
             pltpu.SemaphoreType.DMA((2,)),
@@ -375,10 +370,10 @@
     return pl.pallas_call(
         hand_over,
         out_shape=(shape, shape),
-        in_specs=[anywhere] * 2,
+        in_specs=[pl.BlockSpec(memory_space=pl.ANY)] * 2,
         out_specs=(anywhere, anywhere),
-        scratch_shapes=[pltpu.VMEM((2,) + shape.shape, bf16), pltpu.SemaphoreType.DMA((4,))],
-        compiler_params=pltpu.CompilerParams(vmem_limit_bytes=56 * 1024 * 1024),
+        scratch_shapes=[pltpu.SemaphoreType.DMA((2,))],
+        compiler_params=pltpu.CompilerParams(vmem_limit_bytes=1024 * 1024),
     )(*results)
 
 def solution(mesh):

time: 87.8 us -> 86.9 us (0.990)
  Pallas kernels: 87 us -> 86.1 us
    pallas_call x1, Pallas kernels: 1.77 us -> 0.81 us  [local(): pl.pallas_call(hand_over, out_shape=(shape, shape), in_specs=[pl.BlockSpe...]
where the time goes in v4:
time: 86.9 us; the launch traced here: 86.7 us
  Pallas kernels  86.1 us (99%)
    pallas_call x1, Pallas kernels, local(): pl.pallas_call(partial(kernel, lat_devices, lon_devices, scale, tile), ou...  85.3 us

profile of v4, /device:TPU:1, one launch (start us, length us, event | category | flops | bytes accessed | tf_op | source)
XLA Modules:
  0.0 86.7 jit_solution(9573847595105153285)
XLA Ops:
  0.6 85.3 %shard_map.113 = (bf16[32,16,256]{2,1,0:T(8,128)(2,1)S(1)}, bf16[32,16,256]{2,1,0:T(8,128)(2,1)S(1)}) custom-call(bf16[32,16,256]{2,1,0:T(8,128)(2,1)} %x_in.1, bf16[32,16,256]{2,1,0:T(8,128)(2,1)} %cot_in.1, f32[2,2,2,256,256]{4,3,2,1,0:T(8,128)} %fine_in.1, f32[1,1,2,256,256]{4,3,2,1,0:T(8,128)} %coarse_in.1, bf16[256,1024]{1,0:T(8,128)(2,1)} %w_in_in.1, ...), custom_call_target="tpu_custom_call" | custom-call | tf_op jit(solution)/shard_map/pallas_call | solution.py:354
  85.9 0.8 shard_map.114

commit v5 on v4

--- a/solution.py
+++ b/solution.py
@@ -268,17 +268,14 @@
 
     arrive('lon', 3)
     modes = join_halves(r5[0])
-    for n in range(columns // tile):
-        rows = pl.ds(n * tile, tile)
-        part = pl.ds(n * blocks, blocks)
-        x = xt[part].reshape(tile, channels).astype(f32)
-        m = (x + dot(tt[rows], modes)).astype(bf16)
-        mixed[rows] = m
-        value, slope = gelu_parts(dot(m, w_in[...]))
-        act[rows] = value.astype(bf16)
-        d_hidden = (d_act[rows] * slope).astype(bf16)
-        cot = ct[part].reshape(tile, channels).astype(f32)
-        d_mixed[rows] = (cot + dot_t(d_hidden, w_in[...])).astype(bf16)
+    x = xt[...].reshape(columns, channels).astype(f32)
+    m = (x + dot(tt[...], modes)).astype(bf16)
+    mixed[...] = m
+    value, slope = gelu_parts(dot(m, w_in[...]))
+    act[...] = value.astype(bf16)
+    d_hidden = (d_act[...] * slope).astype(bf16)
+    cot = ct[...].reshape(columns, channels).astype(f32)
+    d_mixed[...] = (cot + dot_t(d_hidden, w_in[...])).astype(bf16)
 
     analysis(d_mixed[...], 1)
     for n in range(columns // tile):
@@ -299,12 +296,28 @@
 
     arrive('lon', 6)
     modes = join_halves(r5[1])
-    for n in range(columns // tile):
-        rows = pl.ds(n * tile, tile)
+    pending.append((grad_ref, send_lon.at[7]))
+    arriving['lon', 7] = (grad_ref, recv_lon.at[7])
+    chunks = max(1, lon_outer // 2)
+    share = lon_devices // chunks
+    for j in range(chunks):
+        away = chunks // 2 + (j + 1) // 2 * (1 - 2 * (j % 2))
+        first = lax.rem(lax.div(k, share) + away, chunks) * share
+        rows = pl.ds(pl.multiple_of(first * 16, share * 16), share * 16)
         value = (d_mixed[rows].astype(f32) + dot(tt[rows], modes)).astype(bf16)
-        grad_rows[pl.ds(n * blocks, blocks)] = value.reshape(blocks, 16, channels)
-
-    send_to_lon(7, grad_rows, grad_ref)
+        grad_rows[pl.ds(first, share)] = value.reshape(share, 16, channels)
+
+        def step(n, _):
+            other = first + n
+
+            @pl.when(other != k)
+            def _():
+                pltpu.make_async_remote_copy(
+                    src_ref=grad_rows.at[other], dst_ref=grad_ref.at[k],
+                    send_sem=send_lon.at[7], recv_sem=recv_lon.at[7],
+                    device_id={"lon": other}, device_id_type=MESH).start()
+            return 0
+        lax.fori_loop(0, share, step, 0)
     own_grad = pltpu.make_async_copy(grad_rows.at[k], grad_ref.at[k], own_sem.at[1])
     own_grad.start()
     opened['grad'] = own_grad
@@ -330,7 +343,7 @@
     rows = row_count * lat_devices
     assert row_count == lon_devices and column_count == 16
     scale = 1.0 / math.sqrt(rows * columns * 4 * lat_devices * lon_devices)
-    tile = min(512, columns)
+    tile = min(128, columns)
     half = channels // 2
     lon_message = (2, lon_devices, 2 * SLOTS, half)
     lat_message = (2, lat_devices, PART, channels)

time: 86.9 us -> 86.6 us (level)
  no operation moved by 1% of the time
where the time goes in v5:
time: 86.6 us; the launch traced here: 86.5 us
  Pallas kernels  85.8 us (99%)
    pallas_call x1, Pallas kernels, local(): pl.pallas_call(partial(kernel, lat_devices, lon_devices, scale, tile), ou...  85 us

profile of v5, /device:TPU:1, one launch (start us, length us, event | category | flops | bytes accessed | tf_op | source)
XLA Modules:
  0.0 86.5 jit_solution(12119689885606182554)
XLA Ops:
  0.6 85.0 %shard_map.113 = (bf16[32,16,256]{2,1,0:T(8,128)(2,1)S(1)}, bf16[32,16,256]{2,1,0:T(8,128)(2,1)S(1)}) custom-call(bf16[32,16,256]{2,1,0:T(8,128)(2,1)} %x_in.1, bf16[32,16,256]{2,1,0:T(8,128)(2,1)} %cot_in.1, f32[2,2,2,256,256]{4,3,2,1,0:T(8,128)} %fine_in.1, f32[1,1,2,256,256]{4,3,2,1,0:T(8,128)} %coarse_in.1, bf16[256,1024]{1,0:T(8,128)(2,1)} %w_in_in.1, ...), custom_call_target="tpu_custom_call" | custom-call | tf_op jit(solution)/shard_map/pallas_call | solution.py:367
  85.7 0.8 shard_map.114

commit v6 on v5

--- a/solution.py
+++ b/solution.py
@@ -127,8 +127,8 @@
             barrier, inc=1, device_id={"lon": lon_partner(j)}, device_id_type=MESH)
         return 0
 
-    lax.fori_loop(0, lat_devices - 1, greet_lat, 0)
-    lax.fori_loop(0, lon_devices - 1, greet_lon, 0)
+    lax.fori_loop(0, lat_devices - 1, greet_lat, 0, unroll=True)
+    lax.fori_loop(0, lon_devices - 1, greet_lon, 0, unroll=True)
     for load in loads[1:]:
         load.start()
     pl.semaphore_wait(barrier, lon_devices + lat_devices - 2)

time: 86.6 us -> 86.3 us (level)
  no operation moved by 1% of the time
where the time goes in v6:
time: 86.3 us; the launch traced here: 86.2 us
  Pallas kernels  85.6 us (99%)
    pallas_call x1, Pallas kernels, local(): pl.pallas_call(partial(kernel, lat_devices, lon_devices, scale, tile), ou...  84.8 us

profile of v6, /device:TPU:1, one launch (start us, length us, event | category | flops | bytes accessed | tf_op | source)
XLA Modules:
  0.0 86.2 jit_solution(17236734458297258435)
XLA Ops:
  0.6 84.8 %shard_map.113 = (bf16[32,16,256]{2,1,0:T(8,128)(2,1)S(1)}, bf16[32,16,256]{2,1,0:T(8,128)(2,1)S(1)}) custom-call(bf16[32,16,256]{2,1,0:T(8,128)(2,1)} %x_in.1, bf16[32,16,256]{2,1,0:T(8,128)(2,1)} %cot_in.1, f32[2,2,2,256,256]{4,3,2,1,0:T(8,128)} %fine_in.1, f32[1,1,2,256,256]{4,3,2,1,0:T(8,128)} %coarse_in.1, bf16[256,1024]{1,0:T(8,128)(2,1)} %w_in_in.1, ...), custom_call_target="tpu_custom_call" | custom-call | tf_op jit(solution)/shard_map/pallas_call | solution.py:367
  85.4 0.8 shard_map.114
